TPU v7x, 32 devices: a whole 2x2x4 slice. The times are simulated.
32 devices in a mesh: expert: 8 (over z, y), segment: 4 (over x, core).
Axes of the slice: x: 2, y: 2, z: 4, core: 2. Of those that a mesh axis runs over, the one named last changes fastest.
Arguments:
- tokens: bfloat16 [4, 8, 128, 1664], P('segment', 'expert'), may hold values from -6 to 6
- route_ids: int32 [4, 8, 128, 2], P('segment', 'expert'), may hold values from 0 to 7, all different within a row; in each aligned block of 128 rows (0 to 127, 128 to 255, ..., all dimensions but the last counted through in order) at most 48 rows name the same one
- cotangent: bfloat16 [4, 8, 128, 1664], P('segment', 'expert'), may hold values from -6 to 6
- first_gain: float32 [1664], replicated, may hold values from 0.25 to 1.75
- in_projection: bfloat16 [1664, 2496], replicated, may hold values from -0.3125 to 0.3125
- out_projection: bfloat16 [832, 1664], replicated, may hold values from -0.21875 to 0.21875
- second_gain: float32 [1664], replicated, may hold values from 0.25 to 1.75
- router_weight: bfloat16 [1664, 8], replicated, may hold values from -0.15625 to 0.15625
- up_weight: bfloat16 [4, 8, 1664, 1024], P('segment', 'expert'), may hold values from -0.15625 to 0.15625
- down_weight: bfloat16 [4, 8, 1024, 1664], P('segment', 'expert'), may hold values from -0.09375 to 0.09375
Outputs:
- layer_out: bfloat16 [4, 8, 128, 1664], P('segment', 'expert')
- input_grad: bfloat16 [4, 8, 128, 1664], P('segment', 'expert')
Inputs may be any that keep to these rules, and one draw needn't show every extreme that they name: `route_ids`: the 2 experts of a token differ; among the 128 tokens of one image no expert is named more than 48 times, and in every draw some image names some expert exactly 48 times.
All inputs are finite; a program needn't handle non-finite values.
Results may differ from a plain program's by a relative error of at most 0.023.
Values may be sent and summed in bfloat16 or wider, within the bound.
No kernel may reach another device: no remote copies, remote signals or barrier semaphores. Data moves between devices by JAX's collectives and lax.ppermute only.
A program may use at most 128 MiB of HBM per device.

v0:
```python
from functools import partial

import jax
import jax.numpy as jnp
from jax import lax
from jax.sharding import PartitionSpec as P

HD = 104
PARTS_SIZE = 4
TOP = 2


EPSILON = 1e-06
ROOT_HALF = 0.7071067811865476
INV_ROOT_TWO_PI = 0.3989422804014327


def passed_along(value, axis, steps):
    count = lax.axis_size(axis)
    pairs = [(source, (source + steps) % count) for source in range(count)]
    return lax.ppermute(value, axis, pairs)


def layer_norm(row_block, gain_vector):
    center = row_block - jnp.mean(row_block, axis=-1, keepdims=True)
    spread = jnp.mean(center * center, axis=-1, keepdims=True)
    return center * lax.rsqrt(spread + EPSILON) * gain_vector


def gelu_exact(preact):
    return 0.5 * preact * (1.0 + lax.erf(preact * ROOT_HALF))


def gelu_slope(preact):
    return 0.5 * (1.0 + lax.erf(preact * ROOT_HALF)) + preact * INV_ROOT_TWO_PI * jnp.exp(
        -0.5 * preact * preact
    )


def attention_branch(picture, first_gain, in_projection, out_projection):
    seq_len = picture.shape[0]
    head_width = out_projection.shape[0]
    head_count = head_width // HD
    normed = layer_norm(picture, first_gain).astype(jnp.bfloat16)
    joined = jnp.dot(normed, in_projection, preferred_element_type=jnp.float32).astype(jnp.bfloat16)
    queries = joined[:, :head_width].reshape(seq_len, head_count, HD)
    key_rows = joined[:, head_width : 2 * head_width].reshape(seq_len, head_count, HD)
    value_rows = joined[:, 2 * head_width :].reshape(seq_len, head_count, HD)
    scores = jnp.einsum(
        "qhd,khd->hqk", queries, key_rows, preferred_element_type=jnp.float32
    ) * HD ** (-0.5)
    weights = jnp.exp(scores)
    attention = (weights / jnp.sum(weights, axis=-1, keepdims=True)).astype(jnp.bfloat16)
    context = jnp.einsum(
        "hqk,khd->qhd", attention, value_rows, preferred_element_type=jnp.float32
    ).astype(jnp.bfloat16)
    return picture + jnp.dot(
        context.reshape(seq_len, head_width), out_projection, preferred_element_type=jnp.float32
    )


def gate_pair(router_input, chosen, router_weight):
    logits = jnp.dot(router_input, router_weight, preferred_element_type=jnp.float32)
    picked = jnp.take_along_axis(logits, chosen, axis=1)
    return 1.0 / (1.0 + jnp.exp(picked[:, ::-1] - picked))


def route_slots(flat_ids, experts):
    onehot = (flat_ids[:, None] == jnp.arange(experts, dtype=jnp.int32)[None, :]).astype(jnp.int32)
    running = jnp.cumsum(onehot, axis=0)
    return jnp.sum(running * onehot, axis=1) - 1


def send_table(row_index, in_section, row_count):
    target = jnp.where(in_section, row_index, -1)
    return (target[None, :] == jnp.arange(row_count, dtype=jnp.int32)[:, None]).astype(jnp.bfloat16)


def prepare(send_rows, router_input, grad_routes):
    slot_count = send_rows.shape[0]
    token_rows = jnp.sum(send_rows.reshape(slot_count, -1, TOP), axis=2)
    mixed_buf = jnp.dot(token_rows, router_input, preferred_element_type=jnp.float32).astype(
        jnp.bfloat16
    )
    grad_buf = jnp.dot(send_rows, grad_routes, preferred_element_type=jnp.float32).astype(
        jnp.bfloat16
    )
    return (token_rows, mixed_buf, grad_buf)


def finish(send_rows, token_rows, out_buf, grad_sum, gate_values, upstream_wide):
    seq_len, model_width = upstream_wide.shape
    picked_out = jnp.einsum(
        "pr,pd->rd", send_rows, out_buf, preferred_element_type=jnp.float32
    ).reshape(seq_len, TOP, model_width)
    expert_add = jnp.sum(gate_values[:, :, None] * picked_out, axis=1)
    gate_add = jnp.sum(upstream_wide[:, None, :] * picked_out, axis=2)
    input_add = jnp.einsum(
        "ps,pd->sd", token_rows.astype(jnp.float32), grad_sum, precision=lax.Precision.HIGHEST
    )
    return (expert_add, gate_add, input_add)


def make_expert(up_local, down_local):

    def compute(received):
        mixed_in, grad_in = received
        layout = mixed_in.shape
        mixed_flat = mixed_in.reshape(-1, layout[-1])
        grad_flat = grad_in.reshape(-1, layout[-1])
        preact = jnp.dot(mixed_flat, up_local, preferred_element_type=jnp.float32)
        hidden = gelu_exact(preact).astype(jnp.bfloat16)
        partial_out = jnp.dot(hidden, down_local, preferred_element_type=jnp.float32).astype(
            jnp.bfloat16
        )
        slope_rows = jnp.einsum(
            "rd,fd->rf", grad_flat, down_local, preferred_element_type=jnp.float32
        ) * gelu_slope(preact)
        hidden_grad = slope_rows.astype(jnp.bfloat16)
        partial_grad = jnp.einsum(
            "rf,df->rd", hidden_grad, up_local, preferred_element_type=jnp.float32
        ).astype(jnp.bfloat16)
        return (partial_out.reshape(layout), partial_grad.reshape(layout))

    return compute


def shards(
    tokens,
    route_ids,
    cotangent,
    first_gain,
    in_projection,
    out_projection,
    second_gain,
    router_weight,
    up_weight,
    down_weight,
):
    picture = tokens[0, 0].astype(jnp.float32)
    chosen = route_ids[0, 0]
    upstream = cotangent[0, 0]
    seq_len, model_width = picture.shape
    experts = router_weight.shape[1]
    segments = lax.axis_size("segment")
    members = lax.axis_size("expert")
    per_section = members // PARTS_SIZE
    capacity = 3 * seq_len // experts
    expert_fn = make_expert(up_weight[0, 0], down_weight[0, 0])

    def branch(row_block):
        return attention_branch(row_block, first_gain, in_projection, out_projection)

    residual, attention_back = jax.vjp(branch, picture)
    normed, norm_back = jax.vjp(partial(layer_norm, gain_vector=second_gain), residual)
    router_input = normed.astype(jnp.bfloat16)
    gate_values = gate_pair(router_input, chosen, router_weight)
    segment_index = lax.axis_index("segment")
    slot_total = per_section * capacity
    carried = (router_input, upstream)
    zero_rows = jnp.zeros((seq_len, model_width), jnp.float32)
    float_carry = (
        zero_rows,
        zero_rows,
        jnp.zeros((seq_len, TOP), jnp.float32),
        gate_values,
        chosen.astype(jnp.float32),
    )
    for visit_index in range(segments):
        visit_input, visit_upstream = carried
        expert_total, input_total, gate_total, visit_gates, visit_ids = float_carry
        flat_ids = visit_ids.astype(jnp.int32).reshape(-1)
        slot_index = route_slots(flat_ids, experts)
        local_ids = flat_ids - segment_index * per_section
        in_section = (local_ids >= 0) & (local_ids < per_section)
        send_rows = send_table(local_ids * capacity + slot_index, in_section, slot_total)
        upstream_wide = visit_upstream.astype(jnp.float32)
        grad_routes = (
            (visit_gates[:, :, None] * upstream_wide[:, None, :])
            .astype(jnp.bfloat16)
            .reshape(-1, model_width)
        )
        token_rows, mixed_buf, grad_buf = prepare(send_rows, visit_input, grad_routes)
        spread_shape = (per_section, PARTS_SIZE, capacity, model_width)
        mixed_send = jnp.broadcast_to(
            mixed_buf.reshape(per_section, 1, capacity, model_width), spread_shape
        ).reshape(members, capacity, model_width)
        grad_send = jnp.broadcast_to(
            grad_buf.reshape(per_section, 1, capacity, model_width), spread_shape
        ).reshape(members, capacity, model_width)
        part_out, part_grad = expert_fn(
            (
                lax.all_to_all(mixed_send, "expert", split_axis=0, concat_axis=0, tiled=True),
                lax.all_to_all(grad_send, "expert", split_axis=0, concat_axis=0, tiled=True),
            )
        )
        back_out, back_grad = (
            lax.all_to_all(part_out, "expert", split_axis=0, concat_axis=0, tiled=True),
            lax.all_to_all(part_grad, "expert", split_axis=0, concat_axis=0, tiled=True),
        )
        out_buf = (
            jnp.sum(back_out.reshape(spread_shape).astype(jnp.float32), axis=1)
            .astype(jnp.bfloat16)
            .reshape(slot_total, model_width)
        )
        grad_sum = jnp.sum(back_grad.reshape(spread_shape).astype(jnp.float32), axis=1).reshape(
            slot_total, model_width
        )
        expert_add, gate_add, input_add = finish(
            send_rows, token_rows, out_buf, grad_sum, visit_gates, upstream_wide
        )
        carried = passed_along((visit_input, visit_upstream), "segment", 1)
        float_carry = (
            passed_along((expert_total + expert_add).astype(jnp.bfloat16), "segment", 1).astype(
                jnp.float32
            ),
            passed_along((input_total + input_add).astype(jnp.bfloat16), "segment", 1).astype(
                jnp.float32
            ),
            passed_along((gate_total + gate_add).astype(jnp.bfloat16), "segment", 1).astype(
                jnp.float32
            ),
            passed_along(visit_gates.astype(jnp.bfloat16), "segment", 1).astype(visit_gates.dtype),
            passed_along(visit_ids.astype(jnp.bfloat16), "segment", 1).astype(visit_ids.dtype),
        )
    expert_total = float_carry[0]
    input_total = float_carry[1]
    gate_total = float_carry[2]
    layer_out = (residual + expert_total).astype(jnp.bfloat16)
    logit_grad = gate_values * (
        gate_total - jnp.sum(gate_values * gate_total, axis=1, keepdims=True)
    )
    choose_table = (
        chosen[:, :, None] == jnp.arange(experts, dtype=jnp.int32)[None, None, :]
    ).astype(jnp.float32)
    spread_grad = jnp.sum(logit_grad[:, :, None] * choose_table, axis=1)
    mixed_grad = input_total + jnp.einsum(
        "se,de->sd", spread_grad, router_weight.astype(jnp.float32), precision=lax.Precision.HIGHEST
    )
    residual_grad = upstream.astype(jnp.float32) + norm_back(mixed_grad)[0]
    input_grad = attention_back(residual_grad)[0].astype(jnp.bfloat16)
    return (layer_out[None, None], input_grad[None, None])


def solution(mesh):
    placed = (
        P("segment", "expert", None, None),
        P("segment", "expert", None, None),
        P("segment", "expert", None, None),
        P(),
        P(),
        P(),
        P(),
        P(),
        P("segment", "expert", None, None),
        P("segment", "expert", None, None),
    )
    return jax.shard_map(
        shards,
        mesh=mesh,
        in_specs=placed,
        out_specs=(P("segment", "expert", None, None), P("segment", "expert", None, None)),
        check_vma=False,
    )
```

profile of v0, /device:TPU:0, one launch (start us, length us, event | category | flops | bytes accessed | tf_op | source)
XLA Modules:
  0.0 615.8 jit_solution(16922016000192003914)
XLA Ops:
  4.9 6.0 convolution_convert_fusion
  20.5 7.4 %all-to-all-start = ((bf16[8,48,1664]{2,1,0:T(8,128)(2,1)}), bf16[8,48,1664]{2,1,0:T(8,128)(2,1)}, u32[]{:S(2)}, u32[]{:S(2)}) async-start(bf16[8,48,1664]{2,1,0:T(8,128)(2,1)} %bitcast.298), calls=%async_computation | async-start | bytes 2555904 | tf_op jit(solution)/shard_map/all_to_all | solution.py:193
  41.5 17.2 %all-to-all-done = bf16[8,48,1664]{2,1,0:T(8,128)(2,1)} async-done(((bf16[8,48,1664]{2,1,0:T(8,128)(2,1)}), bf16[8,48,1664]{2,1,0:T(8,128)(2,1)}, u32[]{:S(2)}, u32[]{:S(2)}) %all-to-all-start) | async-done | bytes 1277984 | tf_op jit(solution)/shard_map/all_to_all | solution.py:193
  75.1 20.4 %all-to-all-done.8 = bf16[8,48,1664]{2,1,0:T(8,128)(2,1)} async-done(((bf16[8,48,1664]{2,1,0:T(8,128)(2,1)}), bf16[8,48,1664]{2,1,0:T(8,128)(2,1)}, u32[]{:S(2)}, u32[]{:S(2)}) %all-to-all-start.8) | async-done | bytes 1277984 | tf_op jit(solution)/shard_map/all_to_all | solution.py:194
  104.3 5.8 collective-permute-done.1
  119.4 13.1 %all-to-all-done.2 = bf16[8,48,1664]{2,1,0:T(8,128)(2,1)} async-done(((bf16[8,48,1664]{2,1,0:T(8,128)(2,1)}), bf16[8,48,1664]{2,1,0:T(8,128)(2,1)}, u32[]{:S(2)}, u32[]{:S(2)}) %all-to-all-start.2) | async-done | bytes 1277984 | tf_op jit(solution)/shard_map/all_to_all | solution.py:193
  145.4 6.4 %collective-permute-done.7 = bf16[128,1664]{1,0:T(8,128)(2,1)} collective-permute-done((bf16[128,1664]{1,0:T(8,128)(2,1)}, bf16[128,1664]{1,0:T(8,128)(2,1)}, u32[]{:S(2)}, u32[]{:S(2)}) %collective-permute-start.7) | collective-permute-done | bytes 426016 | tf_op jit(solution)/shard_map/ppermute | solution.py:21
  153.8 15.6 %all-to-all-done.10 = bf16[8,48,1664]{2,1,0:T(8,128)(2,1)} async-done(((bf16[8,48,1664]{2,1,0:T(8,128)(2,1)}), bf16[8,48,1664]{2,1,0:T(8,128)(2,1)}, u32[]{:S(2)}, u32[]{:S(2)}) %all-to-all-start.10) | async-done | bytes 1277984 | tf_op jit(solution)/shard_map/all_to_all | solution.py:194
  171.5 4.4 all-to-all-start.4
  177.5 6.3 %collective-permute-done.5 = bf16[128,2]{0,1:T(2,128)(2,1)} collective-permute-done((bf16[128,2]{0,1:T(2,128)(2,1)S(1)}, bf16[128,2]{0,1:T(2,128)(2,1)}, u32[]{:S(2)}, u32[]{:S(2)}) %collective-permute-start.5) | collective-permute-done | bytes 544 | tf_op jit(solution)/shard_map/ppermute | solution.py:21
  193.3 12.9 %all-to-all-done.4 = bf16[8,48,1664]{2,1,0:T(8,128)(2,1)} async-done(((bf16[8,48,1664]{2,1,0:T(8,128)(2,1)}), bf16[8,48,1664]{2,1,0:T(8,128)(2,1)}, u32[]{:S(2)}, u32[]{:S(2)}) %all-to-all-start.4) | async-done | bytes 1277984 | tf_op jit(solution)/shard_map/all_to_all | solution.py:193
  221.6 5.1 collective-permute-done.11
  228.7 14.3 %all-to-all-done.12 = bf16[8,48,1664]{2,1,0:T(8,128)(2,1)} async-done(((bf16[8,48,1664]{2,1,0:T(8,128)(2,1)}), bf16[8,48,1664]{2,1,0:T(8,128)(2,1)}, u32[]{:S(2)}, u32[]{:S(2)}) %all-to-all-start.12) | async-done | bytes 1277984 | tf_op jit(solution)/shard_map/all_to_all | solution.py:194
  251.0 6.3 %collective-permute-done.9 = bf16[128,2]{0,1:T(2,128)(2,1)S(1)} collective-permute-done((bf16[128,2]{0,1:T(2,128)(2,1)}, bf16[128,2]{0,1:T(2,128)(2,1)S(1)}, u32[]{:S(2)}, u32[]{:S(2)}) %collective-permute-start.9) | collective-permute-done | bytes 544 | tf_op jit(solution)/shard_map/ppermute | solution.py:21
  266.5 13.1 %all-to-all-done.6 = bf16[8,48,1664]{2,1,0:T(8,128)(2,1)} async-done(((bf16[8,48,1664]{2,1,0:T(8,128)(2,1)}), bf16[8,48,1664]{2,1,0:T(8,128)(2,1)}, u32[]{:S(2)}, u32[]{:S(2)}) %all-to-all-start.6) | async-done | bytes 1277984 | tf_op jit(solution)/shard_map/all_to_all | solution.py:193
  281.8 4.4 all-to-all-start.14
  294.1 22.4 %all-to-all-done.14 = bf16[8,48,1664]{2,1,0:T(8,128)(2,1)} async-done(((bf16[8,48,1664]{2,1,0:T(8,128)(2,1)}), bf16[8,48,1664]{2,1,0:T(8,128)(2,1)}, u32[]{:S(2)}, u32[]{:S(2)}) %all-to-all-start.14) | async-done | bytes 1277984 | tf_op jit(solution)/shard_map/all_to_all | solution.py:194
  320.8 7.1 %fusion.32 = bf16[384,1664]{1,0:T(8,128)(2,1)} fusion(bf16[1,1,1664,1024]{3,2,1,0:T(8,128)(2,1)} %param.18, f32[384,1024]{1,0:T(8,128)} %copy-done.63, bf16[384,1664]{1,0:T(8,128)(2,1)} %bitcast.54, bf16[1,1,1024,1664]{3,2,1,0:T(8,128)(2,1)S(1)} %copy-done), kind=kOutput, calls=%fused_computation.34 | convolution fusion | flops 2621816832 | bytes 10944512 | tf_op jit(solution)/shard_map/rf,df->rd/dot_general | solution.py:120
  327.8 23.2 %all-to-all-done.1 = bf16[8,48,1664]{2,1,0:T(8,128)(2,1)} async-done(((bf16[8,48,1664]{2,1,0:T(8,128)(2,1)}), bf16[8,48,1664]{2,1,0:T(8,128)(2,1)}, u32[]{:S(2)}, u32[]{:S(2)}) %all-to-all-start.1) | async-done | bytes 1277984 | tf_op jit(solution)/shard_map/all_to_all | solution.py:198
  363.2 22.5 %all-to-all-done.9 = bf16[8,48,1664]{2,1,0:T(8,128)(2,1)} async-done(((bf16[8,48,1664]{2,1,0:T(8,128)(2,1)}), bf16[8,48,1664]{2,1,0:T(8,128)(2,1)}, u32[]{:S(2)}, u32[]{:S(2)}) %all-to-all-start.9) | async-done | bytes 1277984 | tf_op jit(solution)/shard_map/all_to_all | solution.py:199
  389.9 7.1 %fusion.35 = bf16[384,1664]{1,0:T(8,128)(2,1)} fusion(bf16[1,1,1664,1024]{3,2,1,0:T(8,128)(2,1)} %param.18, f32[384,1024]{1,0:T(8,128)} %copy-done.64, bf16[384,1664]{1,0:T(8,128)(2,1)} %bitcast.60, bf16[1,1,1024,1664]{3,2,1,0:T(8,128)(2,1)S(1)} %copy-done), kind=kOutput, calls=%fused_computation.35 | convolution fusion | flops 2621816832 | bytes 10944512 | tf_op jit(solution)/shard_map/rf,df->rd/dot_general | solution.py:120
  397.0 23.2 %all-to-all-done.3 = bf16[8,48,1664]{2,1,0:T(8,128)(2,1)} async-done(((bf16[8,48,1664]{2,1,0:T(8,128)(2,1)}), bf16[8,48,1664]{2,1,0:T(8,128)(2,1)}, u32[]{:S(2)}, u32[]{:S(2)}) %all-to-all-start.3) | async-done | bytes 1277984 | tf_op jit(solution)/shard_map/all_to_all | solution.py:198
  420.2 4.5 all-to-all-start.11
  432.5 22.4 %all-to-all-done.11 = bf16[8,48,1664]{2,1,0:T(8,128)(2,1)} async-done(((bf16[8,48,1664]{2,1,0:T(8,128)(2,1)}), bf16[8,48,1664]{2,1,0:T(8,128)(2,1)}, u32[]{:S(2)}, u32[]{:S(2)}) %all-to-all-start.11) | async-done | bytes 1277984 | tf_op jit(solution)/shard_map/all_to_all | solution.py:199
  459.2 7.1 %fusion.38 = bf16[384,1664]{1,0:T(8,128)(2,1)} fusion(bf16[1,1,1664,1024]{3,2,1,0:T(8,128)(2,1)} %param.18, f32[384,1024]{1,0:T(8,128)} %copy-done.65, bf16[384,1664]{1,0:T(8,128)(2,1)} %bitcast.66, bf16[1,1,1024,1664]{3,2,1,0:T(8,128)(2,1)S(1)} %copy-done), kind=kOutput, calls=%fused_computation.36 | convolution fusion | flops 2621816832 | bytes 10944512 | tf_op jit(solution)/shard_map/rf,df->rd/dot_general | solution.py:120
  466.3 23.2 %all-to-all-done.5 = bf16[8,48,1664]{2,1,0:T(8,128)(2,1)} async-done(((bf16[8,48,1664]{2,1,0:T(8,128)(2,1)}), bf16[8,48,1664]{2,1,0:T(8,128)(2,1)}, u32[]{:S(2)}, u32[]{:S(2)}) %all-to-all-start.5) | async-done | bytes 1277984 | tf_op jit(solution)/shard_map/all_to_all | solution.py:198
  506.3 7.1 %fusion.41 = bf16[384,1664]{1,0:T(8,128)(2,1)} fusion(bf16[1,1,1664,1024]{3,2,1,0:T(8,128)(2,1)} %param.18, f32[384,1024]{1,0:T(8,128)} %copy-done.66, bf16[384,1664]{1,0:T(8,128)(2,1)} %bitcast.72, bf16[1,1,1024,1664]{3,2,1,0:T(8,128)(2,1)S(1)} %copy-done), kind=kOutput, calls=%fused_computation.37 | convolution fusion | flops 2621816832 | bytes 10944512 | tf_op jit(solution)/shard_map/rf,df->rd/dot_general | solution.py:120
  517.9 6.2 %all-to-all-done.13 = bf16[8,48,1664]{2,1,0:T(8,128)(2,1)} async-done(((bf16[8,48,1664]{2,1,0:T(8,128)(2,1)}), bf16[8,48,1664]{2,1,0:T(8,128)(2,1)}, u32[]{:S(2)}, u32[]{:S(2)}) %all-to-all-start.13) | async-done | bytes 1277984 | tf_op jit(solution)/shard_map/all_to_all | solution.py:199
  524.1 4.5 all-to-all-start.7
  542.9 16.0 %all-to-all-done.7 = bf16[8,48,1664]{2,1,0:T(8,128)(2,1)} async-done(((bf16[8,48,1664]{2,1,0:T(8,128)(2,1)}), bf16[8,48,1664]{2,1,0:T(8,128)(2,1)}, u32[]{:S(2)}, u32[]{:S(2)}) %all-to-all-start.7) | async-done | bytes 1277984 | tf_op jit(solution)/shard_map/all_to_all | solution.py:198
  574.7 18.8 %all-to-all-done.15 = bf16[8,48,1664]{2,1,0:T(8,128)(2,1)} async-done(((bf16[8,48,1664]{2,1,0:T(8,128)(2,1)}), bf16[8,48,1664]{2,1,0:T(8,128)(2,1)}, u32[]{:S(2)}, u32[]{:S(2)}) %all-to-all-start.15) | async-done | bytes 1277984 | tf_op jit(solution)/shard_map/all_to_all | solution.py:199
  597.0 7.5 %collective-permute-done.19 = bf16[128,1664]{1,0:T(8,128)(2,1)S(1)} collective-permute-done((bf16[128,1664]{1,0:T(8,128)(2,1)S(1)}, bf16[128,1664]{1,0:T(8,128)(2,1)S(1)}, u32[]{:S(2)}, u32[]{:S(2)}) %collective-permute-start.19) | collective-permute-done | bytes 426016 | tf_op jit(solution)/shard_map/ppermute | solution.py:21
  (362 shorter events, 232.0 us)
Async XLA Ops:
  20.5 38.2 %all-to-all-start = ((bf16[8,48,1664]{2,1,0:T(8,128)(2,1)}), bf16[8,48,1664]{2,1,0:T(8,128)(2,1)}, u32[]{:S(2)}, u32[]{:S(2)}) async-start(bf16[8,48,1664]{2,1,0:T(8,128)(2,1)} %bitcast.298), calls=%async_computation | async-start | bytes 2555904 | tf_op jit(solution)/shard_map/all_to_all | solution.py:193
  60.8 34.8 %all-to-all-start.8 = ((bf16[8,48,1664]{2,1,0:T(8,128)(2,1)}), bf16[8,48,1664]{2,1,0:T(8,128)(2,1)}, u32[]{:S(2)}, u32[]{:S(2)}) async-start(bf16[8,48,1664]{2,1,0:T(8,128)(2,1)} %bitcast.296), calls=%async_computation.8 | async-start | bytes 2555904 | tf_op jit(solution)/shard_map/all_to_all | solution.py:194
  65.3 7.9 %collective-permute-start.3 = (bf16[128,1664]{1,0:T(8,128)(2,1)}, bf16[128,1664]{1,0:T(8,128)(2,1)}, u32[]{:S(2)}, u32[]{:S(2)}) collective-permute-start(bf16[128,1664]{1,0:T(8,128)(2,1)} %copy-done.8), channel_id=1, source_target_pairs={{0,1},{1,2},{2,3},{3,0},{4,5},{5,6},{6,7},{7,4},{8,9},{9,10},{10,1... | collective-permute-start | bytes 1277960 | tf_op jit(solution)/shard_map/ppermute | solution.py:21
  97.8 34.7 %all-to-all-start.2 = ((bf16[8,48,1664]{2,1,0:T(8,128)(2,1)}), bf16[8,48,1664]{2,1,0:T(8,128)(2,1)}, u32[]{:S(2)}, u32[]{:S(2)}) async-start(bf16[8,48,1664]{2,1,0:T(8,128)(2,1)} %bitcast.299), calls=%async_computation.2 | async-start | bytes 2555904 | tf_op jit(solution)/shard_map/all_to_all | solution.py:193
  102.2 8.8 %collective-permute-start.14 = (bf16[128,1664]{1,0:T(8,128)(2,1)}, bf16[128,1664]{1,0:T(8,128)(2,1)}, u32[]{:S(2)}, u32[]{:S(2)}) collective-permute-start(bf16[128,1664]{1,0:T(8,128)(2,1)} %bitcast.303), channel_id=1, source_target_pairs={{0,1},{1,2},{2,3},{3,0},{4,5},{5,6},{6,7},{7,4},{8,9},{9,10},{10,1... | collective-permute-start | bytes 1277960 | tf_op jit(solution)/shard_map/ppermute | solution.py:21
  134.7 34.7 %all-to-all-start.10 = ((bf16[8,48,1664]{2,1,0:T(8,128)(2,1)}), bf16[8,48,1664]{2,1,0:T(8,128)(2,1)}, u32[]{:S(2)}, u32[]{:S(2)}) async-start(bf16[8,48,1664]{2,1,0:T(8,128)(2,1)} %bitcast.297), calls=%async_computation.10 | async-start | bytes 2555904 | tf_op jit(solution)/shard_map/all_to_all | solution.py:194
  143.9 7.9 %collective-permute-start.7 = (bf16[128,1664]{1,0:T(8,128)(2,1)}, bf16[128,1664]{1,0:T(8,128)(2,1)}, u32[]{:S(2)}, u32[]{:S(2)}) collective-permute-start(bf16[128,1664]{1,0:T(8,128)(2,1)} %collective-permute-done.3), channel_id=1, source_target_pairs={{0,1},{1,2},{2,3},{3,0},{4,5},{5,6},{6,7},{7,4},{8,9},{9,10},{10,1... | collective-permute-start | bytes 1277960 | tf_op jit(solution)/shard_map/ppermute | solution.py:21
  171.5 34.7 %all-to-all-start.4 = ((bf16[8,48,1664]{2,1,0:T(8,128)(2,1)}), bf16[8,48,1664]{2,1,0:T(8,128)(2,1)}, u32[]{:S(2)}, u32[]{:S(2)}) async-start(bf16[8,48,1664]{2,1,0:T(8,128)(2,1)} %bitcast.300), calls=%async_computation.4 | async-start | bytes 2555904 | tf_op jit(solution)/shard_map/all_to_all | solution.py:193
  175.9 8.9 %collective-permute-start.16 = (bf16[128,1664]{1,0:T(8,128)(2,1)}, bf16[128,1664]{1,0:T(8,128)(2,1)}, u32[]{:S(2)}, u32[]{:S(2)}) collective-permute-start(bf16[128,1664]{1,0:T(8,128)(2,1)} %collective-permute-done.14), channel_id=1, source_target_pairs={{0,1},{1,2},{2,3},{3,0},{4,5},{5,6},{6,7},{7,4},{8,9},{9,10},{10,1... | collective-permute-start | bytes 1277960 | tf_op jit(solution)/shard_map/ppermute | solution.py:21
  176.0 7.9 %collective-permute-start.5 = (bf16[128,2]{0,1:T(2,128)(2,1)S(1)}, bf16[128,2]{0,1:T(2,128)(2,1)}, u32[]{:S(2)}, u32[]{:S(2)}) collective-permute-start(bf16[128,2]{0,1:T(2,128)(2,1)S(1)} %copy-done.49), channel_id=1, source_target_pairs={{0,1},{1,2},{2,3},{3,0},{4,5},{5,6},{6,7},{7,4},{8,9},{9,10},{10,1... | collective-permute-start | bytes 1544 | tf_op jit(solution)/shard_map/ppermute | solution.py:21
  208.3 34.7 %all-to-all-start.12 = ((bf16[8,48,1664]{2,1,0:T(8,128)(2,1)}), bf16[8,48,1664]{2,1,0:T(8,128)(2,1)}, u32[]{:S(2)}, u32[]{:S(2)}) async-start(bf16[8,48,1664]{2,1,0:T(8,128)(2,1)} %bitcast.295), calls=%async_computation.12 | async-start | bytes 2555904 | tf_op jit(solution)/shard_map/all_to_all | solution.py:194
  218.8 7.9 %collective-permute-start.11 = (bf16[128,1664]{1,0:T(8,128)(2,1)}, bf16[128,1664]{1,0:T(8,128)(2,1)}, u32[]{:S(2)}, u32[]{:S(2)}) collective-permute-start(bf16[128,1664]{1,0:T(8,128)(2,1)} %collective-permute-done.7), channel_id=1, source_target_pairs={{0,1},{1,2},{2,3},{3,0},{4,5},{5,6},{6,7},{7,4},{8,9},{9,10},{10,1... | collective-permute-start | bytes 1277960 | tf_op jit(solution)/shard_map/ppermute | solution.py:21
  245.1 34.6 %all-to-all-start.6 = ((bf16[8,48,1664]{2,1,0:T(8,128)(2,1)}), bf16[8,48,1664]{2,1,0:T(8,128)(2,1)}, u32[]{:S(2)}, u32[]{:S(2)}) async-start(bf16[8,48,1664]{2,1,0:T(8,128)(2,1)} %bitcast.301), calls=%async_computation.6 | async-start | bytes 2555904 | tf_op jit(solution)/shard_map/all_to_all | solution.py:193
  249.4 8.7 %collective-permute-start.18 = (bf16[128,1664]{1,0:T(8,128)(2,1)}, bf16[128,1664]{1,0:T(8,128)(2,1)}, u32[]{:S(2)}, u32[]{:S(2)}) collective-permute-start(bf16[128,1664]{1,0:T(8,128)(2,1)} %collective-permute-done.16), channel_id=1, source_target_pairs={{0,1},{1,2},{2,3},{3,0},{4,5},{5,6},{6,7},{7,4},{8,9},{9,10},{10,1... | collective-permute-start | bytes 1277960 | tf_op jit(solution)/shard_map/ppermute | solution.py:21
  281.8 34.7 %all-to-all-start.14 = ((bf16[8,48,1664]{2,1,0:T(8,128)(2,1)}), bf16[8,48,1664]{2,1,0:T(8,128)(2,1)}, u32[]{:S(2)}, u32[]{:S(2)}) async-start(bf16[8,48,1664]{2,1,0:T(8,128)(2,1)} %bitcast.302), calls=%async_computation.14 | async-start | bytes 2555904 | tf_op jit(solution)/shard_map/all_to_all | solution.py:194
  316.5 34.6 %all-to-all-start.1 = ((bf16[8,48,1664]{2,1,0:T(8,128)(2,1)}), bf16[8,48,1664]{2,1,0:T(8,128)(2,1)}, u32[]{:S(2)}, u32[]{:S(2)}) async-start(bf16[8,48,1664]{2,1,0:T(8,128)(2,1)} %bitcast.320), calls=%async_computation.1 | async-start | bytes 2555904 | tf_op jit(solution)/shard_map/all_to_all | solution.py:198
  351.1 34.6 %all-to-all-start.9 = ((bf16[8,48,1664]{2,1,0:T(8,128)(2,1)}), bf16[8,48,1664]{2,1,0:T(8,128)(2,1)}, u32[]{:S(2)}, u32[]{:S(2)}) async-start(bf16[8,48,1664]{2,1,0:T(8,128)(2,1)} %bitcast.318), calls=%async_computation.9 | async-start | bytes 2555904 | tf_op jit(solution)/shard_map/all_to_all | solution.py:199
  385.6 34.6 %all-to-all-start.3 = ((bf16[8,48,1664]{2,1,0:T(8,128)(2,1)}), bf16[8,48,1664]{2,1,0:T(8,128)(2,1)}, u32[]{:S(2)}, u32[]{:S(2)}) async-start(bf16[8,48,1664]{2,1,0:T(8,128)(2,1)} %bitcast.321), calls=%async_computation.3 | async-start | bytes 2555904 | tf_op jit(solution)/shard_map/all_to_all | solution.py:198
  420.2 34.8 %all-to-all-start.11 = ((bf16[8,48,1664]{2,1,0:T(8,128)(2,1)}), bf16[8,48,1664]{2,1,0:T(8,128)(2,1)}, u32[]{:S(2)}, u32[]{:S(2)}) async-start(bf16[8,48,1664]{2,1,0:T(8,128)(2,1)} %bitcast.319), calls=%async_computation.11 | async-start | bytes 2555904 | tf_op jit(solution)/shard_map/all_to_all | solution.py:199
  455.0 34.6 %all-to-all-start.5 = ((bf16[8,48,1664]{2,1,0:T(8,128)(2,1)}), bf16[8,48,1664]{2,1,0:T(8,128)(2,1)}, u32[]{:S(2)}, u32[]{:S(2)}) async-start(bf16[8,48,1664]{2,1,0:T(8,128)(2,1)} %bitcast.322), calls=%async_computation.5 | async-start | bytes 2555904 | tf_op jit(solution)/shard_map/all_to_all | solution.py:198
  489.5 34.6 %all-to-all-start.13 = ((bf16[8,48,1664]{2,1,0:T(8,128)(2,1)}), bf16[8,48,1664]{2,1,0:T(8,128)(2,1)}, u32[]{:S(2)}, u32[]{:S(2)}) async-start(bf16[8,48,1664]{2,1,0:T(8,128)(2,1)} %bitcast.317), calls=%async_computation.13 | async-start | bytes 2555904 | tf_op jit(solution)/shard_map/all_to_all | solution.py:199
  516.3 16.6 %collective-permute-start = (bf16[128,1664]{1,0:T(8,128)(2,1)}, bf16[128,1664]{1,0:T(8,128)(2,1)}, u32[]{:S(2)}, u32[]{:S(2)}) collective-permute-start(bf16[128,1664]{1,0:T(8,128)(2,1)} %get-tuple-element.3), channel_id=1, source_target_pairs={{0,1},{1,2},{2,3},{3,0},{4,5},{5,6},{6,7},{7,4},{8,9},{9,10},{10,1... | collective-permute-start | bytes 1277960 | tf_op jit(solution)/shard_map/ppermute | solution.py:21
  516.3 20.0 %collective-permute-start.20 = (bf16[128,2]{0,1:T(2,128)(2,1)S(1)}, bf16[128,2]{0,1:T(2,128)(2,1)S(1)}, u32[]{:S(2)}, u32[]{:S(2)}) collective-permute-start(bf16[128,2]{0,1:T(2,128)(2,1)S(1)} %get-tuple-element.2), channel_id=1, source_target_pairs={{0,1},{1,2},{2,3},{3,0},{4,5},{5,6},{6,7},{7,4},{8,9},{9,10},{10,1... | collective-permute-start | bytes 1544 | tf_op jit(solution)/shard_map/ppermute | solution.py:21
  524.1 34.8 %all-to-all-start.7 = ((bf16[8,48,1664]{2,1,0:T(8,128)(2,1)}), bf16[8,48,1664]{2,1,0:T(8,128)(2,1)}, u32[]{:S(2)}, u32[]{:S(2)}) async-start(bf16[8,48,1664]{2,1,0:T(8,128)(2,1)} %bitcast.316), calls=%async_computation.7 | async-start | bytes 2555904 | tf_op jit(solution)/shard_map/all_to_all | solution.py:198
  534.7 28.4 %collective-permute-start.4 = (bf16[128,1664]{1,0:T(8,128)(2,1)}, bf16[128,1664]{1,0:T(8,128)(2,1)}, u32[]{:S(2)}, u32[]{:S(2)}) collective-permute-start(bf16[128,1664]{1,0:T(8,128)(2,1)} %add_convert_fusion.7), channel_id=1, source_target_pairs={{0,1},{1,2},{2,3},{3,0},{4,5},{5,6},{6,7},{7,4},{8,9},{9,10},{10,1... | collective-permute-start | bytes 1277960 | tf_op jit(solution)/shard_map/ppermute | solution.py:21
  536.3 28.3 %collective-permute-start.21 = (bf16[128,2]{0,1:T(2,128)(2,1)S(1)}, bf16[128,2]{0,1:T(2,128)(2,1)S(1)}, u32[]{:S(2)}, u32[]{:S(2)}) collective-permute-start(bf16[128,2]{0,1:T(2,128)(2,1)S(1)} %add_convert_fusion.10), channel_id=1, source_target_pairs={{0,1},{1,2},{2,3},{3,0},{4,5},{5,6},{6,7},{7,4},{8,9},{9,10},{10,1... | collective-permute-start | bytes 1544 | tf_op jit(solution)/shard_map/ppermute | solution.py:21
  539.7 28.1 %collective-permute-start.15 = (bf16[128,1664]{1,0:T(8,128)(2,1)}, bf16[128,1664]{1,0:T(8,128)(2,1)}, u32[]{:S(2)}, u32[]{:S(2)}) collective-permute-start(bf16[128,1664]{1,0:T(8,128)(2,1)} %add_convert_fusion.3), channel_id=1, source_target_pairs={{0,1},{1,2},{2,3},{3,0},{4,5},{5,6},{6,7},{7,4},{8,9},{9,10},{10,1... | collective-permute-start | bytes 1277960 | tf_op jit(solution)/shard_map/ppermute | solution.py:21
  558.9 34.6 %all-to-all-start.15 = ((bf16[8,48,1664]{2,1,0:T(8,128)(2,1)}), bf16[8,48,1664]{2,1,0:T(8,128)(2,1)}, u32[]{:S(2)}, u32[]{:S(2)}) async-start(bf16[8,48,1664]{2,1,0:T(8,128)(2,1)} %bitcast.315), calls=%async_computation.15 | async-start | bytes 2555904 | tf_op jit(solution)/shard_map/all_to_all | solution.py:199
  564.6 9.2 %collective-permute-start.22 = (bf16[128,2]{0,1:T(2,128)(2,1)S(1)}, bf16[128,2]{0,1:T(2,128)(2,1)S(1)}, u32[]{:S(2)}, u32[]{:S(2)}) collective-permute-start(bf16[128,2]{0,1:T(2,128)(2,1)S(1)} %add_convert_fusion.9), channel_id=1, source_target_pairs={{0,1},{1,2},{2,3},{3,0},{4,5},{5,6},{6,7},{7,4},{8,9},{9,10},{10,1... | collective-permute-start | bytes 1544 | tf_op jit(solution)/shard_map/ppermute | solution.py:21
  570.2 24.9 %collective-permute-start.17 = (bf16[128,1664]{1,0:T(8,128)(2,1)}, bf16[128,1664]{1,0:T(8,128)(2,1)}, u32[]{:S(2)}, u32[]{:S(2)}) collective-permute-start(bf16[128,1664]{1,0:T(8,128)(2,1)} %add_convert_fusion.2), channel_id=1, source_target_pairs={{0,1},{1,2},{2,3},{3,0},{4,5},{5,6},{6,7},{7,4},{8,9},{9,10},{10,1... | collective-permute-start | bytes 1277960 | tf_op jit(solution)/shard_map/ppermute | solution.py:21
  573.2 32.1 %collective-permute-start.12 = (bf16[128,1664]{1,0:T(8,128)(2,1)}, bf16[128,1664]{1,0:T(8,128)(2,1)}, u32[]{:S(2)}, u32[]{:S(2)}) collective-permute-start(bf16[128,1664]{1,0:T(8,128)(2,1)} %add_convert_fusion.5), channel_id=1, source_target_pairs={{0,1},{1,2},{2,3},{3,0},{4,5},{5,6},{6,7},{7,4},{8,9},{9,10},{10,1... | collective-permute-start | bytes 1277960 | tf_op jit(solution)/shard_map/ppermute | solution.py:21
  573.8 23.1 %collective-permute-start.23 = (bf16[128,2]{0,1:T(2,128)(2,1)S(1)}, bf16[128,2]{0,1:T(2,128)(2,1)S(1)}, u32[]{:S(2)}, u32[]{:S(2)}) collective-permute-start(bf16[128,2]{0,1:T(2,128)(2,1)S(1)} %add_convert_fusion.8), channel_id=1, source_target_pairs={{0,1},{1,2},{2,3},{3,0},{4,5},{5,6},{6,7},{7,4},{8,9},{9,10},{10,1... | collective-permute-start | bytes 1544 | tf_op jit(solution)/shard_map/ppermute | solution.py:21
  (77 other events, 734.1 us)
where the time goes:
time: 626 us; the launch traced here: 616 us
  waiting for transfers between devices  333 us (53%)
  matrix products  93.2 us (15%)
  starting transfers between devices  86.6 us (14%)
  local copies, waits for them, and re-layouts  59.7 us (10%)
  other arithmetic  41 us (7%)
    all_to_all x4, waiting for transfers between devices, shards(): lax.all_to_all(part_out, 'expert', split_axis=0, concat_axis=0, tiled=True)  85.7 us
    all_to_all x4, waiting for transfers between devices, shards(): lax.all_to_all(grad_send, 'expert', split_axis=0, concat_axis=0, tiled=True)  72.7 us
    all_to_all x4, waiting for transfers between devices, shards(): lax.all_to_all(part_grad, 'expert', split_axis=0, concat_axis=0, tiled=True)  69.8 us
    all_to_all x4, waiting for transfers between devices, shards(): lax.all_to_all(mixed_send, 'expert', split_axis=0, concat_axis=0, tiled=T...  56.3 us
    ppermute x24, waiting for transfers between devices, passed_along(): return lax.ppermute(value, axis, pairs)  48.4 us
    dot_general x4, matrix products, compute(): jnp.einsum('rf,df->rd', hidden_grad, up_local, preferred_element_type=jnp...  28.3 us
    mul x8, local copies, waits for them, and re-layouts, shards(): visit_gates[:, :, None] * upstream_wide[:, None, :]  22.9 us
    all_to_all x4, starting transfers between devices, shards(): lax.all_to_all(mixed_send, 'expert', split_axis=0, concat_axis=0, tiled=T...  20.5 us
  transfers between devices with their start and end apart: 40, of which 27 were waited for; matrix products, arithmetic and copies ran while one was open for 23% of the time, Pallas kernels for 0%

commit v1 on v0

v1 whole, which is shorter than its diff:
```python
from functools import partial

import jax
import jax.numpy as jnp
from jax import lax
from jax.sharding import PartitionSpec as P

HD = 104
PARTS_SIZE = 4
TOP = 2


EPSILON = 1e-06
ROOT_HALF = 0.7071067811865476
INV_ROOT_TWO_PI = 0.3989422804014327


def layer_norm(row_block, gain_vector):
    center = row_block - jnp.mean(row_block, axis=-1, keepdims=True)
    spread = jnp.mean(center * center, axis=-1, keepdims=True)
    return center * lax.rsqrt(spread + EPSILON) * gain_vector


def gelu_parts(preact):
    half_cdf = 0.5 * (1.0 + lax.erf(preact * ROOT_HALF))
    slope = half_cdf + preact * INV_ROOT_TWO_PI * jnp.exp(-0.5 * preact * preact)
    return preact * half_cdf, slope


def attention_branch(picture, first_gain, in_projection, out_projection):
    seq_len = picture.shape[0]
    head_width = out_projection.shape[0]
    head_count = head_width // HD
    normed = layer_norm(picture, first_gain).astype(jnp.bfloat16)
    joined = jnp.dot(normed, in_projection, preferred_element_type=jnp.float32).astype(jnp.bfloat16)
    queries = joined[:, :head_width].reshape(seq_len, head_count, HD)
    key_rows = joined[:, head_width : 2 * head_width].reshape(seq_len, head_count, HD)
    value_rows = joined[:, 2 * head_width :].reshape(seq_len, head_count, HD)
    scores = jnp.einsum(
        "qhd,khd->hqk", queries, key_rows, preferred_element_type=jnp.float32
    ) * HD ** (-0.5)
    weights = jnp.exp(scores)
    attention = (weights / jnp.sum(weights, axis=-1, keepdims=True)).astype(jnp.bfloat16)
    context = jnp.einsum(
        "hqk,khd->qhd", attention, value_rows, preferred_element_type=jnp.float32
    ).astype(jnp.bfloat16)
    return picture + jnp.dot(
        context.reshape(seq_len, head_width), out_projection, preferred_element_type=jnp.float32
    )


def slot_of(hits):
    seq_len = hits.shape[-1]
    order = jnp.arange(seq_len)
    before = (order[:, None] < order[None, :]).astype(jnp.bfloat16)
    return jnp.dot(
        hits.astype(jnp.bfloat16), before, preferred_element_type=jnp.float32
    ).astype(jnp.int32)


def row_table(ids, experts_here, capacity):
    images, seq_len, _ = ids.shape
    hits = jnp.any(ids[None] == experts_here[:, None, None, None], axis=-1)
    sections = hits.shape[0]
    slots = slot_of(hits.reshape(-1, seq_len)).reshape(hits.shape)
    rows = slots + jnp.arange(images)[None, :, None] * capacity
    rows = jnp.where(hits, rows, -1).reshape(sections, 1, images * seq_len)
    return (rows == jnp.arange(images * capacity)[None, :, None]).astype(jnp.bfloat16)


def shards(
    tokens,
    route_ids,
    cotangent,
    first_gain,
    in_projection,
    out_projection,
    second_gain,
    router_weight,
    up_weight,
    down_weight,
):
    picture = tokens[0, 0].astype(jnp.float32)
    chosen = route_ids[0, 0]
    upstream = cotangent[0, 0]
    up_local = up_weight[0, 0]
    down_local = down_weight[0, 0]
    seq_len, width = picture.shape
    experts = router_weight.shape[1]
    sections = lax.axis_size("segment")
    members = lax.axis_size("expert")
    per_section = members // PARTS_SIZE
    capacity = 3 * seq_len // experts
    line = members // 2
    here = lax.axis_index("expert")
    section = lax.axis_index("segment")
    place, side = here // 2, here % 2
    group = here // PARTS_SIZE
    my_expert = section * per_section + group
    experts_here = jnp.arange(sections) * per_section + group

    def along(value, steps):
        pairs = [(j, (j + 2 * steps) % members) for j in range(members)]
        return lax.ppermute(value, "expert", pairs)

    def across(value):
        return lax.ppermute(value, "expert", [(j, j ^ 1) for j in range(members)])

    def deal(value):
        return lax.all_to_all(value, "segment", split_axis=0, concat_axis=0, tiled=True)

    half = line // 2
    chunks = [list(range(1, half + 1)), list(range(half + 1, line)) + [0]]

    all_ids = lax.all_gather(chosen, ("segment", "expert")).reshape(
        sections, members, seq_len, TOP
    )
    lane_ids = lax.dynamic_index_in_dim(all_ids, section, 0, keepdims=False)

    def sources(chunk):
        spots = (place - jnp.array(chunk)) % line
        return jnp.concatenate([2 * spots + side, 2 * spots + 1 - side])

    cot_dense = {0: upstream}
    for step in range(1, line):
        cot_dense[step] = along(upstream, step)
    tables, cot_rows = {}, {}
    for index in (1, 0):
        chunk = chunks[index]
        count = len(chunk)
        ids = jnp.take(lane_ids, sources(chunk), axis=0)
        tables[index] = (
            row_table(ids[:count], experts_here, capacity),
            row_table(ids[count:], experts_here, capacity),
        )
        dense = jnp.concatenate([cot_dense[step] for step in chunk], axis=0)
        packed = jnp.einsum(
            "srt,td->srd", tables[index][0], dense, preferred_element_type=jnp.float32
        ).astype(jnp.bfloat16)
        mine = deal(packed)
        cot_rows[index] = jnp.stack([mine, across(mine)], axis=1)

    def branch(row_block):
        return attention_branch(row_block, first_gain, in_projection, out_projection)

    residual, attention_back = jax.vjp(branch, picture)
    normed, norm_back = jax.vjp(partial(layer_norm, gain_vector=second_gain), residual)
    mixed = normed.astype(jnp.bfloat16)
    own_logits = jnp.dot(mixed, router_weight, preferred_element_type=jnp.float32)

    mixed_dense = {0: mixed}
    for step in range(1, line):
        mixed_dense[step] = along(mixed, step)

    out_dense, grad_dense, scores = {}, {}, {}
    for index in (0, 1):
        chunk = chunks[index]
        count = len(chunk)
        rows = count * capacity
        near, far = tables[index]
        dense = jnp.concatenate([mixed_dense[step] for step in chunk], axis=0)
        dense_far = across(dense)
        packed = jnp.stack(
            [
                jnp.einsum("srt,td->srd", table, block, preferred_element_type=jnp.float32)
                for table, block in ((near, dense), (far, dense_far))
            ],
            axis=1,
        ).astype(jnp.bfloat16)
        mixed_rows = deal(packed).reshape(-1, width)
        grads_in = cot_rows[index].reshape(-1, width)

        ids = jnp.take(all_ids, sources(chunk), axis=1)
        hits = jnp.any(ids == my_expert, axis=-1)
        slots = jnp.where(
            hits, slot_of(hits.reshape(-1, seq_len)).reshape(hits.shape), -1
        )
        others = jnp.sum(ids, axis=-1) - my_expert
        slot_hits = slots[:, :, None, :] == jnp.arange(capacity)[None, None, :, None]
        slot_other = jnp.sum(jnp.where(slot_hits, others[:, :, None, :], 0), axis=-1).reshape(-1)

        logits = jnp.dot(mixed_rows, router_weight, preferred_element_type=jnp.float32)
        lanes = jnp.arange(experts)
        mine_logit = jnp.sum(jnp.where(lanes[None, :] == my_expert, logits, 0.0), axis=1)
        other_logit = jnp.sum(jnp.where(lanes[None, :] == slot_other[:, None], logits, 0.0), axis=1)
        gate = (1.0 / (1.0 + jnp.exp(other_logit - mine_logit)))[:, None]

        preact = jnp.dot(mixed_rows, up_local, preferred_element_type=jnp.float32)
        hidden_wide, slope = gelu_parts(preact)
        hidden = hidden_wide.astype(jnp.bfloat16)
        out_rows = (
            jnp.dot(hidden, down_local, preferred_element_type=jnp.float32) * gate
        ).astype(jnp.bfloat16)
        pulled = (
            jnp.einsum("rd,fd->rf", grads_in, down_local, preferred_element_type=jnp.float32)
            * gate
        )
        scores[index] = jnp.sum(hidden.astype(jnp.float32) * pulled, axis=1)
        hidden_grad = (pulled * slope).astype(jnp.bfloat16)
        grad_rows = jnp.einsum(
            "rf,df->rd", hidden_grad, up_local, preferred_element_type=jnp.float32
        ).astype(jnp.bfloat16)

        out_rows = out_rows.reshape(sections, 2, rows, width)
        met = across(out_rows[:, 1])
        summed = (out_rows[:, 0].astype(jnp.float32) + met.astype(jnp.float32)).astype(jnp.bfloat16)
        back = deal(summed)
        out_block = jnp.einsum(
            "srt,srd->td", near, back, preferred_element_type=jnp.float32
        )
        back = deal(grad_rows.reshape(sections, 2, rows, width))
        grad_far = jnp.einsum(
            "srt,srd->td", far, back[:, 1], preferred_element_type=jnp.float32
        ).astype(jnp.bfloat16)
        grad_near = jnp.einsum("srt,srd->td", near, back[:, 0], preferred_element_type=jnp.float32)
        grad_block = grad_near + across(grad_far).astype(jnp.float32)
        for spot, step in enumerate(chunk):
            part_out = out_block[spot * seq_len : (spot + 1) * seq_len]
            part_grad = grad_block[spot * seq_len : (spot + 1) * seq_len]
            if step:
                part_out = along(part_out.astype(jnp.bfloat16), -step)
                part_grad = along(part_grad.astype(jnp.bfloat16), -step)
            out_dense[step] = part_out
            grad_dense[step] = part_grad

    expert_total = sum(out_dense[step].astype(jnp.float32) for step in range(line))
    input_total = sum(grad_dense[step].astype(jnp.float32) for step in range(line))
    layer_out = (residual + expert_total).astype(jnp.bfloat16)

    score_table = jnp.concatenate(
        [scores[index].reshape(sections, 2, len(chunks[index]), capacity) for index in (0, 1)],
        axis=2,
    )
    spot_of = {step: spot for spot, step in enumerate(chunks[0] + chunks[1])}
    spots = jnp.array([spot_of[step] for step in range(line)])
    all_scores = lax.all_gather(score_table, ("segment", "expert")).reshape(
        sections, members, sections, 2, line, capacity
    )
    all_scores = lax.dynamic_index_in_dim(all_scores, section, 2, keepdims=False)
    member = jnp.arange(members)
    pick_side = (member % 2 != side).astype(jnp.int32)
    pick_spot = spots[(member // 2 - place) % line]
    picked = all_scores[:, member, pick_side, pick_spot]
    expert_scores = jnp.sum(
        picked.reshape(sections, per_section, PARTS_SIZE, capacity), axis=2
    ).reshape(experts, capacity)
    expert_list = jnp.arange(experts)
    named = chosen[:, :, None] == expert_list
    hits = jnp.any(named, axis=1)
    own_slots = slot_of(hits.T)
    at_slot = (own_slots[:, :, None] == jnp.arange(capacity)) & hits.T[:, :, None]
    token_scores = jnp.sum(jnp.where(at_slot, expert_scores[:, None, :], 0.0), axis=2).T
    picked_logit = jnp.sum(jnp.where(named, own_logits[:, None, :], 0.0), axis=2)
    gate_values = 1.0 / (1.0 + jnp.exp(picked_logit[:, ::-1] - picked_logit))
    gate_spread = jnp.sum(jnp.where(named, gate_values[:, :, None], 0.0), axis=1)
    spread_grad = token_scores - gate_spread * jnp.sum(token_scores, axis=1, keepdims=True)
    mixed_grad = input_total + jnp.einsum(
        "se,de->sd", spread_grad, router_weight.astype(jnp.float32), precision=lax.Precision.HIGHEST
    )
    residual_grad = upstream.astype(jnp.float32) + norm_back(mixed_grad)[0]
    input_grad = attention_back(residual_grad)[0].astype(jnp.bfloat16)
    return (layer_out[None, None], input_grad[None, None])


def solution(mesh):
    placed = (
        P("segment", "expert", None, None),
        P("segment", "expert", None, None),
        P("segment", "expert", None, None),
        P(),
        P(),
        P(),
        P(),
        P(),
        P("segment", "expert", None, None),
        P("segment", "expert", None, None),
    )
    return jax.shard_map(
        shards,
        mesh=mesh,
        in_specs=placed,
        out_specs=(P("segment", "expert", None, None), P("segment", "expert", None, None)),
        check_vma=False,
    )
```

time: 626 us -> 573 us (0.915)
  the two profiles are of different devices: /device:TPU:0 before, /device:TPU:20 now
where the time goes in v1:
time: 573 us; the launch traced here: 564 us
  blocking collectives  182 us (32%)
  waiting for transfers between devices  170 us (30%)
  matrix products  89.2 us (16%)
  starting transfers between devices  66.5 us (12%)
  local copies, waits for them, and re-layouts  29 us (5%)
  other arithmetic  24.8 us (4%)
    all_gather x1, blocking collectives, shards(): lax.all_gather(chosen, ('segment', 'expert'))  94.7 us
    ppermute x8, waiting for transfers between devices, across(): return lax.ppermute(value, 'expert', [(j, j ^ 1) for j in range(members)])  90.7 us
    all_gather x1, blocking collectives, shards(): lax.all_gather(score_table, ('segment', 'expert'))  87.6 us
    ppermute x12, waiting for transfers between devices, along(): return lax.ppermute(value, 'expert', pairs)  52.1 us
    all_to_all x8, starting transfers between devices, deal(): lax.all_to_all(value, 'segment', split_axis=0, concat_axis=0, tiled=True)  35.8 us
    all_to_all x8, waiting for transfers between devices, deal(): lax.all_to_all(value, 'segment', split_axis=0, concat_axis=0, tiled=True)  27.3 us
    ppermute x12, starting transfers between devices, along(): return lax.ppermute(value, 'expert', pairs)  18.1 us
    ppermute x8, starting transfers between devices, across(): return lax.ppermute(value, 'expert', [(j, j ^ 1) for j in range(members)])  12.6 us
  transfers between devices with their start and end apart: 28, of which 16 were waited for; matrix products, arithmetic and copies ran while one was open for 20% of the time, Pallas kernels for 0%

profile of v1, /device:TPU:20, one launch (start us, length us, event | category | flops | bytes accessed | tf_op | source)
XLA Modules:
  0.0 563.7 jit_solution(4207513081819376520)
XLA Ops:
  7.3 6.0 %convolution_convert_fusion = bf16[128,2496]{0,1:T(8,128)(2,1)S(1)} fusion(bf16[1664,2496]{0,1:T(8,128)(2,1)} %param.23, bf16[1,1,128,1664]{3,2,1,0:T(8,128)(2,1)} %param.19, f32[1664]{0:T(1024)} %param.22, f32[128]{0:T(128)S(1)} %fusion.119, f32[128]{0:T(128)S(1)} %broadcast_multiply_fusion.1), kind=kOutput, calls=%fused_computation.10 | convolution fusion | flops 1064640512 | bytes 9379328 | tf_op jit(solution)/shard_map/jvp()/dot_general | solution.py:35
  21.3 94.7 %all-gather = s32[32,1,128,2]{2,3,1,0:T(2,128)S(1)} all-gather(s32[1,1,128,2]{2,3,1,0:T(2,128)S(1)} %copy-done.25), channel_id=2, replica_groups=mesh['expert'=8,'segment'=4] {'segment','expert'}, dimensions={0}, use_global_device_ids=true | all-gather | bytes 33792 | tf_op jit(solution)/shard_map/all_gather | solution.py:115
  128.7 4.3 all-to-all-start.6
  142.0 8.0 %all-to-all-done.6 = bf16[4,96,1664]{2,1,0:T(8,128)(2,1)} async-done(((bf16[4,96,1664]{2,1,0:T(8,128)(2,1)}), bf16[4,96,1664]{2,1,0:T(8,128)(2,1)}, u32[]{:S(2)}, u32[]{:S(2)}) %all-to-all-start.6) | async-done | bytes 1277984 | tf_op jit(solution)/shard_map/all_to_all | solution.py:110
  150.0 4.3 all-to-all-start.4
  162.5 8.8 %all-to-all-done.4 = bf16[4,96,1664]{2,1,0:T(8,128)(2,1)} async-done(((bf16[4,96,1664]{2,1,0:T(8,128)(2,1)}), bf16[4,96,1664]{2,1,0:T(8,128)(2,1)}, u32[]{:S(2)}, u32[]{:S(2)}) %all-to-all-start.4) | async-done | bytes 1277984 | tf_op jit(solution)/shard_map/all_to_all | solution.py:110
  171.3 4.6 all-to-all-start
  187.8 15.0 %collective-permute-done.5 = bf16[256,1664]{1,0:T(8,128)(2,1)} collective-permute-done((bf16[256,1664]{1,0:T(8,128)(2,1)}, bf16[256,1664]{1,0:T(8,128)(2,1)}, u32[]{:S(2)}, u32[]{:S(2)}) %collective-permute-start.5) | collective-permute-done | bytes 852000 | tf_op jit(solution)/shard_map/ppermute | solution.py:107
  206.5 4.7 all-to-all-start.2
  211.3 18.8 %collective-permute-done.11 = bf16[4,96,1664]{2,1,0:T(8,128)(2,1)} collective-permute-done((bf16[4,96,1664]{2,1,0:T(8,128)(2,1)}, bf16[4,96,1664]{2,1,0:T(8,128)(2,1)}, u32[]{:S(2)}, u32[]{:S(2)}) %collective-permute-start.11) | collective-permute-done | bytes 1277984 | tf_op jit(solution)/shard_map/ppermute | solution.py:107
  233.7 23.5 %collective-permute-done.15 = bf16[4,96,1664]{2,1,0:T(8,128)(2,1)} collective-permute-done((bf16[4,96,1664]{2,1,0:T(8,128)(2,1)}, bf16[4,96,1664]{2,1,0:T(8,128)(2,1)}, u32[]{:S(2)}, u32[]{:S(2)}) %collective-permute-start.15) | collective-permute-done | bytes 1277984 | tf_op jit(solution)/shard_map/ppermute | solution.py:107
  263.6 6.4 %fusion.12 = f32[768,1024]{1,0:T(8,128)} fusion(bf16[768,1664]{1,0:T(8,128)(2,1)} %bitcast.15, bf16[1,1,1664,1024]{3,2,1,0:T(8,128)(2,1)S(1)} %copy-done.34), kind=kOutput, calls=%fused_computation.23 | convolution fusion | flops 2617245696 | bytes 9109504 | tf_op jit(solution)/shard_map/dot_general | solution.py:188
  270.1 5.7 %fusion.10 = f32[768,1024]{1,0:T(8,128)S(1)} fusion(bf16[768,1664]{1,0:T(8,128)(2,1)} %bitcast.31, bf16[1,1,1664,1024]{3,2,1,0:T(8,128)(2,1)} %param.27), kind=kOutput, calls=%fused_computation.21 | convolution fusion | flops 2617245696 | bytes 9109504 | tf_op jit(solution)/shard_map/dot_general | solution.py:188
  278.5 4.6 multiply_reduce_fusion.1
  283.1 5.5 fusion.17
  288.6 4.8 all-to-all-start.7
  293.4 6.2 %multiply_reduce_fusion = (f32[768]{0:T(1024)S(1)}, bf16[768,1024]{1,0:T(8,128)(2,1)S(1)}, f32[768,1024]{1,0:T(8,128)S(1)}) fusion(f32[768]{0:T(1024)S(1)} %add_divide_fusion.1, f32[768,1024]{1,0:T(8,128)} %fusion.12, bf16[768,1664]{1,0:T(8,128)(2,1)} %bitcast.279, bf16[1,1,1024,1664]{3,2,1,0:T(8,128)(2,1)S(1)} %copy-done), kind=kOutput, calls=%fused_computation.37 | convolution fusion | flops 2624322816 | bytes 13834240 | tf_op jit(solution)/shard_map/rd,fd->rf/dot_general | solution.py:195
  299.6 4.3 multiply_convert_fusion
  303.9 4.3 multiply_convert_fusion.1
  308.2 5.6 fusion.14
  313.7 10.3 %all-to-all-done.7 = bf16[4,2,96,1664]{3,2,1,0:T(8,128)(2,1)} async-done(((bf16[4,2,96,1664]{3,2,1,0:T(8,128)(2,1)}), bf16[4,2,96,1664]{3,2,1,0:T(8,128)(2,1)}, u32[]{:S(2)}, u32[]{:S(2)}) %all-to-all-start.7) | async-done | bytes 2555936 | tf_op jit(solution)/shard_map/all_to_all | solution.py:110
  324.0 4.5 all-to-all-start.5
  333.0 87.6 %all-gather.1 = f32[128,2,4,48]{3,2,1,0:T(4,128)S(1)} all-gather(f32[4,2,4,48]{3,2,1,0:T(4,128)S(1)} %pad_maximum_fusion.5), channel_id=3, replica_groups=mesh['expert'=8,'segment'=4] {'segment','expert'}, dimensions={0}, use_global_device_ids=true | all-gather | bytes 202752 | tf_op jit(solution)/shard_map/all_gather | solution.py:236
  430.2 4.3 all-to-all-start.3
  439.6 15.7 %collective-permute-done.2 = bf16[4,96,1664]{2,1,0:T(8,128)(2,1)} collective-permute-done((bf16[4,96,1664]{2,1,0:T(8,128)(2,1)}, bf16[4,96,1664]{2,1,0:T(8,128)(2,1)}, u32[]{:S(2)}, u32[]{:S(2)}) %collective-permute-start.2) | collective-permute-done | bytes 1277984 | tf_op jit(solution)/shard_map/ppermute | solution.py:107
  460.9 4.3 all-to-all-start.1
  467.2 6.4 %collective-permute-done.16 = bf16[256,1664]{1,0:T(8,128)(2,1)} collective-permute-done((bf16[256,1664]{1,0:T(8,128)(2,1)}, bf16[256,1664]{1,0:T(8,128)(2,1)}, u32[]{:S(2)}, u32[]{:S(2)}) %collective-permute-start.16) | collective-permute-done | bytes 852000 | tf_op jit(solution)/shard_map/ppermute | solution.py:107
  480.5 8.4 %collective-permute-done.12 = bf16[256,1664]{1,0:T(8,128)(2,1)} collective-permute-done((bf16[256,1664]{1,0:T(8,128)(2,1)}, bf16[256,1664]{1,0:T(8,128)(2,1)}, u32[]{:S(2)}, u32[]{:S(2)}) %collective-permute-start.12) | collective-permute-done | bytes 852000 | tf_op jit(solution)/shard_map/ppermute | solution.py:107
  500.9 10.7 %collective-permute-done.18 = bf16[128,1664]{1,0:T(8,128)(2,1)} collective-permute-done((bf16[128,1664]{1,0:T(8,128)(2,1)}, bf16[128,1664]{1,0:T(8,128)(2,1)}, u32[]{:S(2)}, u32[]{:S(2)}) %collective-permute-start.18) | collective-permute-done | bytes 426016 | tf_op jit(solution)/shard_map/ppermute | solution.py:104
  511.6 25.7 %collective-permute-done.19 = bf16[128,1664]{1,0:T(8,128)(2,1)} collective-permute-done((bf16[128,1664]{1,0:T(8,128)(2,1)}, bf16[128,1664]{1,0:T(8,128)(2,1)}, u32[]{:S(2)}, u32[]{:S(2)}) %collective-permute-start.19) | collective-permute-done | bytes 426016 | tf_op jit(solution)/shard_map/ppermute | solution.py:104
  539.1 7.9 %collective-permute-done.8 = bf16[128,1664]{1,0:T(8,128)(2,1)} collective-permute-done((bf16[128,1664]{1,0:T(8,128)(2,1)}, bf16[128,1664]{1,0:T(8,128)(2,1)}, u32[]{:S(2)}, u32[]{:S(2)}) %collective-permute-start.8) | collective-permute-done | bytes 426016 | tf_op jit(solution)/shard_map/ppermute | solution.py:104
  547.0 7.8 %collective-permute-done.9 = bf16[128,1664]{1,0:T(8,128)(2,1)S(1)} collective-permute-done((bf16[128,1664]{1,0:T(8,128)(2,1)S(1)}, bf16[128,1664]{1,0:T(8,128)(2,1)S(1)}, u32[]{:S(2)}, u32[]{:S(2)}) %collective-permute-start.9) | collective-permute-done | bytes 426016 | tf_op jit(solution)/shard_map/ppermute | solution.py:104
  (263 shorter events, 128.3 us)
Async XLA Ops:
  0.6 277.9 %copy-start = (bf16[1,1,1024,1664]{3,2,1,0:T(8,128)(2,1)S(1)}, bf16[1,1,1024,1664]{3,2,1,0:T(8,128)(2,1)}, u32[]{:S(2)}) copy-start(bf16[1,1,1024,1664]{3,2,1,0:T(8,128)(2,1)} %param.28) | copy-start | bytes 10223620
  0.6 122.0 %collective-permute-start.13 = (bf16[128,1664]{1,0:T(8,128)(2,1)}, bf16[128,1664]{1,0:T(8,128)(2,1)}, u32[]{:S(2)}, u32[]{:S(2)}) collective-permute-start(bf16[128,1664]{1,0:T(8,128)(2,1)} %bitcast.286), channel_id=1, source_target_pairs={{0,8},{4,12},{8,16},{12,20},{16,24},{20,28},{24,0},{28,4},{1,9},{5... | collective-permute-start | bytes 1277960 | tf_op jit(solution)/shard_map/ppermute | solution.py:104
  2.3 137.0 %collective-permute-start.10 = (bf16[128,1664]{1,0:T(8,128)(2,1)}, bf16[128,1664]{1,0:T(8,128)(2,1)}, u32[]{:S(2)}, u32[]{:S(2)}) collective-permute-start(bf16[128,1664]{1,0:T(8,128)(2,1)} %bitcast.287), channel_id=1, source_target_pairs={{0,24},{4,28},{8,0},{12,4},{16,8},{20,12},{24,16},{28,20},{1,25},{... | collective-permute-start | bytes 1277960 | tf_op jit(solution)/shard_map/ppermute | solution.py:104
  2.7 123.2 %collective-permute-start.14 = (bf16[128,1664]{1,0:T(8,128)(2,1)}, bf16[128,1664]{1,0:T(8,128)(2,1)}, u32[]{:S(2)}, u32[]{:S(2)}) collective-permute-start(bf16[128,1664]{1,0:T(8,128)(2,1)} %bitcast.288), channel_id=1, source_target_pairs={{0,16},{4,20},{8,24},{12,28},{16,0},{20,4},{24,8},{28,12},{1,17},{... | collective-permute-start | bytes 1277960 | tf_op jit(solution)/shard_map/ppermute | solution.py:104
  18.3 159.4 %collective-permute-start.4 = (bf16[128,1664]{1,0:T(8,128)(2,1)}, bf16[128,1664]{1,0:T(8,128)(2,1)}, u32[]{:S(2)}, u32[]{:S(2)}) collective-permute-start(bf16[128,1664]{1,0:T(8,128)(2,1)} %multiply_convert_fusion.4), channel_id=1, source_target_pairs={{0,16},{4,20},{8,24},{12,28},{16,0},{20,4},{24,8},{28,12},{1,17},{... | collective-permute-start | bytes 1277960 | tf_op jit(solution)/shard_map/ppermute | solution.py:104
  19.1 156.8 %collective-permute-start.3 = (bf16[128,1664]{1,0:T(8,128)(2,1)}, bf16[128,1664]{1,0:T(8,128)(2,1)}, u32[]{:S(2)}, u32[]{:S(2)}) collective-permute-start(bf16[128,1664]{1,0:T(8,128)(2,1)} %multiply_convert_fusion.4), channel_id=1, source_target_pairs={{0,8},{4,12},{8,16},{12,20},{16,24},{20,28},{24,0},{28,4},{1,9},{5... | collective-permute-start | bytes 1277960 | tf_op jit(solution)/shard_map/ppermute | solution.py:104
  122.6 10.6 %collective-permute-start = (bf16[128,1664]{1,0:T(8,128)(2,1)}, bf16[128,1664]{1,0:T(8,128)(2,1)}, u32[]{:S(2)}, u32[]{:S(2)}) collective-permute-start(bf16[128,1664]{1,0:T(8,128)(2,1)} %multiply_convert_fusion.4), channel_id=1, source_target_pairs={{0,24},{4,28},{8,0},{12,4},{16,8},{20,12},{24,16},{28,20},{1,25},{... | collective-permute-start | bytes 1277960 | tf_op jit(solution)/shard_map/ppermute | solution.py:104
  128.7 21.3 %all-to-all-start.6 = ((bf16[4,96,1664]{2,1,0:T(8,128)(2,1)}), bf16[4,96,1664]{2,1,0:T(8,128)(2,1)}, u32[]{:S(2)}, u32[]{:S(2)}) async-start(bf16[4,96,1664]{2,1,0:T(8,128)(2,1)} %convolution_convert_fusion.1), calls=%async_computation.6 | async-start | bytes 2555904 | tf_op jit(solution)/shard_map/all_to_all | solution.py:110
  135.3 23.5 %collective-permute-start.1 = (bf16[256,1664]{1,0:T(8,128)(2,1)}, bf16[256,1664]{1,0:T(8,128)(2,1)}, u32[]{:S(2)}, u32[]{:S(2)}) collective-permute-start(bf16[256,1664]{1,0:T(8,128)(2,1)} %pad_maximum_fusion.4), channel_id=1, source_target_pairs={{0,4},{4,0},{8,12},{12,8},{16,20},{20,16},{24,28},{28,24},{1,5},{5... | collective-permute-start | bytes 2555912 | tf_op jit(solution)/shard_map/ppermute | solution.py:107
  150.0 21.3 %all-to-all-start.4 = ((bf16[4,96,1664]{2,1,0:T(8,128)(2,1)}), bf16[4,96,1664]{2,1,0:T(8,128)(2,1)}, u32[]{:S(2)}, u32[]{:S(2)}) async-start(bf16[4,96,1664]{2,1,0:T(8,128)(2,1)} %convolution_convert_fusion.2), calls=%async_computation.4 | async-start | bytes 2555904 | tf_op jit(solution)/shard_map/all_to_all | solution.py:110
  171.3 35.2 %all-to-all-start = ((bf16[4,2,96,1664]{3,2,1,0:T(8,128)(2,1)}), bf16[4,2,96,1664]{3,2,1,0:T(8,128)(2,1)}, u32[]{:S(2)}, u32[]{:S(2)}) async-start(bf16[4,2,96,1664]{3,2,1,0:T(8,128)(2,1)} %copy.164), calls=%async_computation | async-start | bytes 5111808 | tf_op jit(solution)/shard_map/all_to_all | solution.py:110
  179.5 23.2 %collective-permute-start.5 = (bf16[256,1664]{1,0:T(8,128)(2,1)}, bf16[256,1664]{1,0:T(8,128)(2,1)}, u32[]{:S(2)}, u32[]{:S(2)}) collective-permute-start(bf16[256,1664]{1,0:T(8,128)(2,1)} %constant_dynamic-update-slice_fusion), channel_id=1, source_target_pairs={{0,4},{4,0},{8,12},{12,8},{16,20},{20,16},{24,28},{28,24},{1,5},{5... | collective-permute-start | bytes 2555912 | tf_op jit(solution)/shard_map/ppermute | solution.py:107
  183.8 46.3 %collective-permute-start.11 = (bf16[4,96,1664]{2,1,0:T(8,128)(2,1)}, bf16[4,96,1664]{2,1,0:T(8,128)(2,1)}, u32[]{:S(2)}, u32[]{:S(2)}) collective-permute-start(bf16[4,96,1664]{2,1,0:T(8,128)(2,1)} %all-to-all-done.4), channel_id=1, source_target_pairs={{0,4},{4,0},{8,12},{12,8},{16,20},{20,16},{24,28},{28,24},{1,5},{5... | collective-permute-start | bytes 3833864 | tf_op jit(solution)/shard_map/ppermute | solution.py:107
  183.8 73.4 %collective-permute-start.15 = (bf16[4,96,1664]{2,1,0:T(8,128)(2,1)}, bf16[4,96,1664]{2,1,0:T(8,128)(2,1)}, u32[]{:S(2)}, u32[]{:S(2)}) collective-permute-start(bf16[4,96,1664]{2,1,0:T(8,128)(2,1)} %all-to-all-done.6), channel_id=1, source_target_pairs={{0,4},{4,0},{8,12},{12,8},{16,20},{20,16},{24,28},{28,24},{1,5},{5... | collective-permute-start | bytes 3833864 | tf_op jit(solution)/shard_map/ppermute | solution.py:107
  206.5 63.5 %all-to-all-start.2 = ((bf16[4,2,96,1664]{3,2,1,0:T(8,128)(2,1)}), bf16[4,2,96,1664]{3,2,1,0:T(8,128)(2,1)}, u32[]{:S(2)}, u32[]{:S(2)}) async-start(bf16[4,2,96,1664]{3,2,1,0:T(8,128)(2,1)} %copy.173), calls=%async_computation.2 | async-start | bytes 5111808 | tf_op jit(solution)/shard_map/all_to_all | solution.py:110
  288.6 35.4 %all-to-all-start.7 = ((bf16[4,2,96,1664]{3,2,1,0:T(8,128)(2,1)}), bf16[4,2,96,1664]{3,2,1,0:T(8,128)(2,1)}, u32[]{:S(2)}, u32[]{:S(2)}) async-start(bf16[4,2,96,1664]{3,2,1,0:T(8,128)(2,1)} %bitcast.281), calls=%async_computation.7 | async-start | bytes 5111808 | tf_op jit(solution)/shard_map/all_to_all | solution.py:110
  324.0 106.1 %all-to-all-start.5 = ((bf16[4,2,96,1664]{3,2,1,0:T(8,128)(2,1)}), bf16[4,2,96,1664]{3,2,1,0:T(8,128)(2,1)}, u32[]{:S(2)}, u32[]{:S(2)}) async-start(bf16[4,2,96,1664]{3,2,1,0:T(8,128)(2,1)} %bitcast.278), calls=%async_computation.5 | async-start | bytes 5111808 | tf_op jit(solution)/shard_map/all_to_all | solution.py:110
  331.2 95.9 %collective-permute-start.6 = (bf16[4,96,1664]{2,1,0:T(8,128)(2,1)}, bf16[4,96,1664]{2,1,0:T(8,128)(2,1)}, u32[]{:S(2)}, u32[]{:S(2)}) collective-permute-start(bf16[4,96,1664]{2,1,0:T(8,128)(2,1)} %slice_bitcast_fusion.12), channel_id=1, source_target_pairs={{0,4},{4,0},{8,12},{12,8},{16,20},{20,16},{24,28},{28,24},{1,5},{5... | collective-permute-start | bytes 3833864 | tf_op jit(solution)/shard_map/ppermute | solution.py:107
  424.0 31.3 %collective-permute-start.2 = (bf16[4,96,1664]{2,1,0:T(8,128)(2,1)}, bf16[4,96,1664]{2,1,0:T(8,128)(2,1)}, u32[]{:S(2)}, u32[]{:S(2)}) collective-permute-start(bf16[4,96,1664]{2,1,0:T(8,128)(2,1)} %slice_bitcast_fusion.14), channel_id=1, source_target_pairs={{0,4},{4,0},{8,12},{12,8},{16,20},{20,16},{24,28},{28,24},{1,5},{5... | collective-permute-start | bytes 3833864 | tf_op jit(solution)/shard_map/ppermute | solution.py:107
  430.2 30.8 %all-to-all-start.3 = ((bf16[4,96,1664]{2,1,0:T(8,128)(2,1)}), bf16[4,96,1664]{2,1,0:T(8,128)(2,1)}, u32[]{:S(2)}, u32[]{:S(2)}) async-start(bf16[4,96,1664]{2,1,0:T(8,128)(2,1)} %fusion.37), calls=%async_computation.3 | async-start | bytes 2555904 | tf_op jit(solution)/shard_map/all_to_all | solution.py:110
  437.6 36.0 %collective-permute-start.16 = (bf16[256,1664]{1,0:T(8,128)(2,1)}, bf16[256,1664]{1,0:T(8,128)(2,1)}, u32[]{:S(2)}, u32[]{:S(2)}) collective-permute-start(bf16[256,1664]{1,0:T(8,128)(2,1)} %fusion.36), channel_id=1, source_target_pairs={{0,4},{4,0},{8,12},{12,8},{16,20},{20,16},{24,28},{28,24},{1,5},{5... | collective-permute-start | bytes 2555912 | tf_op jit(solution)/shard_map/ppermute | solution.py:107
  460.9 28.0 %collective-permute-start.12 = (bf16[256,1664]{1,0:T(8,128)(2,1)}, bf16[256,1664]{1,0:T(8,128)(2,1)}, u32[]{:S(2)}, u32[]{:S(2)}) collective-permute-start(bf16[256,1664]{1,0:T(8,128)(2,1)} %fusion.35), channel_id=1, source_target_pairs={{0,4},{4,0},{8,12},{12,8},{16,20},{20,16},{24,28},{28,24},{1,5},{5... | collective-permute-start | bytes 2555912 | tf_op jit(solution)/shard_map/ppermute | solution.py:107
  460.9 37.6 %all-to-all-start.1 = ((bf16[4,96,1664]{2,1,0:T(8,128)(2,1)}), bf16[4,96,1664]{2,1,0:T(8,128)(2,1)}, u32[]{:S(2)}, u32[]{:S(2)}) async-start(bf16[4,96,1664]{2,1,0:T(8,128)(2,1)} %fusion.38), calls=%async_computation.1 | async-start | bytes 2555904 | tf_op jit(solution)/shard_map/all_to_all | solution.py:110
  476.8 24.0 %collective-permute-start.17 = (bf16[128,1664]{1,0:T(8,128)(2,1)}, bf16[128,1664]{1,0:T(8,128)(2,1)}, u32[]{:S(2)}, u32[]{:S(2)}) collective-permute-start(bf16[128,1664]{1,0:T(8,128)(2,1)} %get-tuple-element.33), channel_id=1, source_target_pairs={{0,24},{4,28},{8,0},{12,4},{16,8},{20,12},{24,16},{28,20},{1,25},{... | collective-permute-start | bytes 1277960 | tf_op jit(solution)/shard_map/ppermute | solution.py:104
  477.0 34.5 %collective-permute-start.18 = (bf16[128,1664]{1,0:T(8,128)(2,1)}, bf16[128,1664]{1,0:T(8,128)(2,1)}, u32[]{:S(2)}, u32[]{:S(2)}) collective-permute-start(bf16[128,1664]{1,0:T(8,128)(2,1)} %get-tuple-element.34), channel_id=1, source_target_pairs={{0,16},{4,20},{8,24},{12,28},{16,0},{20,4},{24,8},{28,12},{1,17},{... | collective-permute-start | bytes 1277960 | tf_op jit(solution)/shard_map/ppermute | solution.py:104
  493.2 44.0 %collective-permute-start.19 = (bf16[128,1664]{1,0:T(8,128)(2,1)}, bf16[128,1664]{1,0:T(8,128)(2,1)}, u32[]{:S(2)}, u32[]{:S(2)}) collective-permute-start(bf16[128,1664]{1,0:T(8,128)(2,1)} %slice.176), channel_id=1, source_target_pairs={{0,8},{4,12},{8,16},{12,20},{16,24},{20,28},{24,0},{28,4},{1,9},{5... | collective-permute-start | bytes 1277960 | tf_op jit(solution)/shard_map/ppermute | solution.py:104
  494.2 45.0 %collective-permute-start.7 = (bf16[128,1664]{1,0:T(8,128)(2,1)}, bf16[128,1664]{1,0:T(8,128)(2,1)}, u32[]{:S(2)}, u32[]{:S(2)}) collective-permute-start(bf16[128,1664]{1,0:T(8,128)(2,1)} %get-tuple-element.35), channel_id=1, source_target_pairs={{0,24},{4,28},{8,0},{12,4},{16,8},{20,12},{24,16},{28,20},{1,25},{... | collective-permute-start | bytes 1277960 | tf_op jit(solution)/shard_map/ppermute | solution.py:104
  496.2 50.8 %collective-permute-start.8 = (bf16[128,1664]{1,0:T(8,128)(2,1)}, bf16[128,1664]{1,0:T(8,128)(2,1)}, u32[]{:S(2)}, u32[]{:S(2)}) collective-permute-start(bf16[128,1664]{1,0:T(8,128)(2,1)} %get-tuple-element.36), channel_id=1, source_target_pairs={{0,16},{4,20},{8,24},{12,28},{16,0},{20,4},{24,8},{28,12},{1,17},{... | collective-permute-start | bytes 1277960 | tf_op jit(solution)/shard_map/ppermute | solution.py:104
  498.6 38.7 %copy-start.9 = (f32[256,1664]{1,0:T(8,128)S(1)}, f32[256,1664]{1,0:T(8,128)}, u32[]{:S(2)}) copy-start(f32[256,1664]{1,0:T(8,128)} %copy-done.8) | copy-start | bytes 5111812
  498.6 38.7 %copy-start.10 = (f32[128,1664]{1,0:T(8,128)S(1)}, f32[128,1664]{1,0:T(8,128)}, u32[]{:S(2)}) copy-start(f32[128,1664]{1,0:T(8,128)} %fusion.102) | copy-start | bytes 2555908
  500.8 54.0 %copy-start.27 = (f32[128]{0:T(128)S(1)}, f32[128]{0:T(128)}, u32[]{:S(2)}) copy-start(f32[128]{0:T(128)} %copy-done.26) | copy-start | bytes 1540
  500.8 54.0 %collective-permute-start.9 = (bf16[128,1664]{1,0:T(8,128)(2,1)S(1)}, bf16[128,1664]{1,0:T(8,128)(2,1)S(1)}, u32[]{:S(2)}, u32[]{:S(2)}) collective-permute-start(bf16[128,1664]{1,0:T(8,128)(2,1)S(1)} %slice.177), channel_id=1, source_target_pairs={{0,8},{4,12},{8,16},{12,20},{16,24},{20,28},{24,0},{28,4},{1,9},{5... | collective-permute-start | bytes 1277960 | tf_op jit(solution)/shard_map/ppermute | solution.py:104
  (38 other events, 234.3 us)
